TPU v7x, 32 devices: a whole 2x2x4 slice. The times are simulated.
32 devices in a mesh: row: 8 (over z, x), col: 4 (over y, core).
Axes of the slice: x: 2, y: 2, z: 4, core: 2. Of those that a mesh axis runs over, the one named last changes fastest.
Arguments:
- a_vals: float32 [8, 4, 448, 4096], P('row', 'col'), may hold values from -0.1875 to 0.1875
- a_row: int32 [8, 4, 448], P('row', 'col'), may hold values from 0 to 31
- a_col: int32 [8, 4, 448], P('row', 'col'), may hold values from 0 to 63
- a_slot: int32 [8, 4, 3, 448], P('row', 'col'), may hold values from 0 to 5
- a_count: int32 [8, 4], P('row', 'col'), may hold values from 1 to 448, as said below
- p_vals: float32 [256, 3, 4096], P(('row', 'col')), may hold values from -0.75 to 0.75
- p_owner: int32 [256, 3], P(('row', 'col')), may hold values from 0 to 7, all different within a row; in each aligned block of 8 rows (0 to 7, 8 to 15, ...) at most 4 rows name the same one
- p_sub: int32 [256, 3], P(('row', 'col')), may hold values from 0 to 3
- ap_cslot: int32 [256, 3, 6], P(('row', 'col')), may hold values from 0 to 26
Outputs:
- coarse: float32 [32, 27, 4096], P(('row', 'col'))
Inputs may be any that keep to these rules, and one draw needn't show every extreme that they name: `a_count`: at least one device holds exactly 448 listed blocks. `p_owner`: the 3 entries of a fine block row differ; among the rows of one device each row group is named at most 4 times.
All inputs are finite; a program needn't handle non-finite values.
Results may differ from a plain program's by a relative error of at most 0.0001.
Values sent between devices are 32-bit elements; how exact they have to be, the bound alone decides.
A program may use at most 128 MiB of HBM per device.

v0:
```python
import jax
import jax.numpy as jnp
from jax import lax
from jax.sharding import PartitionSpec as P

BLOCK = 64
CPD = 1
TAP = 6
TC = 27


highest = lax.Precision.HIGHEST
tile_batch = 16


def on_device(a_vals, a_row, a_col, a_slot, a_count, p_vals, p_owner, p_sub, ap_cslot):
    row_devices = lax.axis_size("row")
    col_devices = lax.axis_size("col")
    capacity = a_vals.shape[2]
    rows_dev = p_vals.shape[0]
    branches = p_vals.shape[1]
    tile_len = p_vals.shape[2]
    group_rows = rows_dev * col_devices
    group_coarse = CPD * col_devices
    per_peer = max(2, 3 * rows_dev * branches // (2 * row_devices))
    matrix_tiles = a_vals.reshape(capacity, BLOCK, BLOCK)
    tile_rows = a_row.reshape(capacity)
    tile_cols = a_col.reshape(capacity)
    tile_slots = a_slot.reshape(branches, capacity)
    tile_count = a_count.reshape(())
    panel = lax.all_gather(p_vals, "row", axis=0, tiled=True)
    panel_tiles = panel.reshape(rows_dev * row_devices, branches, BLOCK, BLOCK)

    def add_batch(batch_index, partial_value):
        first_tile = batch_index * tile_batch
        block_tiles = lax.dynamic_slice_in_dim(matrix_tiles, first_tile, tile_batch, 0)
        block_rows = lax.dynamic_slice_in_dim(tile_rows, first_tile, tile_batch, 0)
        block_cols = lax.dynamic_slice_in_dim(tile_cols, first_tile, tile_batch, 0)
        block_slots = lax.dynamic_slice_in_dim(tile_slots, first_tile, tile_batch, 1)
        right_tiles = jnp.take(panel_tiles, block_cols, axis=0)
        products = jnp.einsum("tij,tsjk->tsik", block_tiles, right_tiles, precision=highest)
        is_live = first_tile + jnp.arange(tile_batch, dtype=jnp.int32) < tile_count
        products = jnp.where(is_live[:, None, None, None], products, 0.0)
        target = block_rows[:, None] * TAP + block_slots.T
        return partial_value.at[target.reshape(-1)].add(
            products.reshape(tile_batch * branches, tile_len)
        )

    batches = (tile_count + tile_batch - 1) // tile_batch
    partial_value = lax.fori_loop(
        0, batches, add_batch, jnp.zeros((group_rows * TAP, tile_len), jnp.float32)
    )
    ap_rows = lax.psum_scatter(
        partial_value.reshape(group_rows, TAP, tile_len), "col", scatter_dimension=0, tiled=True
    )
    item_count = rows_dev * branches
    owners = p_owner.reshape(item_count)
    serial = jnp.arange(item_count, dtype=jnp.int32)
    earlier = (owners[:, None] == owners[None, :]) & (serial[None, :] < serial[:, None])
    placed = owners * per_peer + jnp.sum(earlier.astype(jnp.int32), axis=1)
    slots_total = row_devices * per_peer
    metadata = jnp.concatenate(
        [p_sub.reshape(item_count, 1), ap_cslot.reshape(item_count, TAP)], axis=1
    ).astype(jnp.float32)
    meta_send = jnp.zeros((slots_total, TAP + 1), jnp.float32).at[placed].set(metadata)
    ap_items = jnp.broadcast_to(ap_rows[:, None], (rows_dev, branches, TAP, tile_len)).reshape(
        item_count, TAP, tile_len
    )
    packed = jnp.concatenate([p_vals.reshape(item_count, 1, tile_len), ap_items], axis=1)
    outgoing = jnp.zeros((slots_total, TAP + 1, tile_len), jnp.float32).at[placed].set(packed)
    incoming, meta_in = (
        lax.all_to_all(outgoing, "row", split_axis=0, concat_axis=0, tiled=True),
        lax.all_to_all(meta_send, "row", split_axis=0, concat_axis=0, tiled=True),
    )
    left_in = incoming[:, 0].reshape(slots_total, BLOCK, BLOCK)
    right_in = incoming[:, 1:].reshape(slots_total, TAP, BLOCK, BLOCK)
    arrived = jnp.einsum("ejk,eqjl->eqkl", left_in, right_in, precision=highest).reshape(
        slots_total, TAP, tile_len
    )
    arrived_index = meta_in.astype(jnp.int32)
    target = arrived_index[:, :1] * TC + arrived_index[:, 1:]
    coarse_part = (
        jnp.zeros((group_coarse * TC, tile_len), jnp.float32)
        .at[target.reshape(-1)]
        .add(arrived.reshape(slots_total * TAP, tile_len))
    )
    coarse = lax.psum_scatter(
        coarse_part.reshape(group_coarse, TC, tile_len), "col", scatter_dimension=0, tiled=True
    )
    return coarse


def solution(mesh):
    placed = (
        P("row", "col", None, None),
        P("row", "col", None),
        P("row", "col", None),
        P("row", "col", None, None),
        P("row", "col"),
        P(("row", "col"), None, None),
        P(("row", "col"), None),
        P(("row", "col"), None),
        P(("row", "col"), None, None),
    )
    return jax.shard_map(
        on_device,
        mesh=mesh,
        in_specs=placed,
        out_specs=P(("row", "col"), None, None),
        check_vma=False,
    )
```

profile of v0, /device:TPU:0, one launch (start us, length us, event | category | flops | bytes accessed | tf_op | source)
XLA Modules:
  0.0 943.6 jit_solution(4953588879980151144)
XLA Ops:
  8.0 9.0 copy.62
  17.0 11.9 %copy.64 = f32[448,64,64]{2,1,0:T(8,128)} copy(f32[448,64,64]{0,2,1:T(8,128)} %bitcast.50) | data formatting | bytes 14680064 | tf_op jit(solution)/shard_map/while | solution.py:50
  29.0 43.8 %all-gather.2.cloned.1.call-done = f32[64,3,4096]{2,0,1:T(8,128)} async-done(((f32[8,3,4096]{2,0,1:T(8,128)}), f32[64,3,4096]{2,0,1:T(8,128)}) %all-gather.2.cloned.1.call-update) | async-done | bytes 3145744 | tf_op jit(solution)/shard_map/all_gather | solution.py:31
  72.8 6.1 reshape.159
  78.9 6.5 copy.63
  85.7 325.6 %while.10 = (s32[]{:T(128)}, f32[192,4096]{1,0:T(8,128)S(1)}, s32[]{:T(128)}, s32[448]{0:T(512)}, s32[3,448]{0,1:T(8,128)S(1)}, /*index=5*/s32[]{:T(128)}, s32[4...) while((s32[]{:T(128)}, f32[192,4096]{1,0:T(8,128)S(1)}, ...), condition=%wide.region_4.5_spmd, body=%wide.region_2.4_spmd.sunk | while | flops 151586128 | bytes 9967619 | solution.py:50
  87.2 4.6 gather_fusion
  91.8 5.5 select_bitcast_fusion.2
  108.9 4.6 gather_fusion
  113.5 5.5 select_bitcast_fusion.2
  130.6 4.6 gather_fusion
  135.2 5.5 select_bitcast_fusion.2
  152.3 4.6 gather_fusion
  156.9 5.5 select_bitcast_fusion.2
  174.0 4.6 gather_fusion
  178.6 5.5 select_bitcast_fusion.2
  195.7 4.6 gather_fusion
  200.3 5.5 select_bitcast_fusion.2
  217.4 4.6 gather_fusion
  222.0 5.5 select_bitcast_fusion.2
  239.1 4.6 gather_fusion
  243.7 5.5 select_bitcast_fusion.2
  260.8 4.6 gather_fusion
  265.4 5.5 select_bitcast_fusion.2
  282.5 4.6 gather_fusion
  287.1 5.5 select_bitcast_fusion.2
  304.2 4.6 gather_fusion
  308.8 5.5 select_bitcast_fusion.2
  325.9 4.6 gather_fusion
  330.5 5.5 select_bitcast_fusion.2
  347.6 4.6 gather_fusion
  352.2 5.5 select_bitcast_fusion.2
  369.3 4.6 gather_fusion
  374.0 5.5 select_bitcast_fusion.2
  391.0 4.6 gather_fusion
  395.7 5.5 select_bitcast_fusion.2
  416.4 285.4 %all-to-all-start = ((f32[8,4,7]{2,1,0:T(4,128)}), f32[8,4,7]{2,1,0:T(4,128)S(1)}, u32[]{:S(2)}, u32[]{:S(2)}) async-start(f32[8,4,7]{2,1,0:T(4,128)} %bitcast.7), calls=%async_computation | async-start | bytes 32768 | tf_op jit(solution)/shard_map/all_to_all | solution.py:73
  702.3 36.7 %reduce-scatter.3.cloned.1.call-done = f32[8,6,4096]{2,1,0:T(8,128)} async-done(((f32[32,6,4096]{2,1,0:T(8,128)}), f32[8,6,4096]{2,1,0:T(8,128)}) %reduce-scatter.3.cloned.1.call-update) | async-done | bytes 786448 | tf_op jit(solution)/shard_map/reduce_scatter | solution.py:53
  750.0 6.7 scatter_fusion.1
  756.7 5.6 all-to-all-start.1
  762.7 92.8 %all-to-all-done.1 = f32[32,7,4096]{2,1,0:T(8,128)} async-done(((f32[32,7,4096]{2,1,0:T(8,128)}), f32[32,7,4096]{2,1,0:T(8,128)}, u32[]{:S(2)}, u32[]{:S(2)}) %all-to-all-start.1) | async-done | bytes 3670048 | tf_op jit(solution)/shard_map/all_to_all | solution.py:72
  855.5 5.1 slice.20
  860.6 6.8 reshape.208
  871.4 13.2 %convolution_bitcast_fusion = f32[32,6,64,64]{2,3,1,0:T(8,128)} fusion(f32[32,6,64,64]{3,2,1,0:T(8,128)} %reshape.208, f32[32,64,64,1]{2,1,0,3:T(8,128)S(1)} %reshape.207), kind=kOutput, calls=%fused_computation.23 | convolution fusion | flops 603979776 | bytes 6815744 | tf_op jit(solution)/shard_map/ejk,eqjl->eqkl/dot_general | solution.py:77
  884.6 6.6 copy.69
  891.2 5.9 reshape.201
  897.1 6.3 scatter_custom_fusion.3
  905.1 29.7 %reduce-scatter.5.cloned.1.call-done = f32[1,27,4096]{2,1,0:T(8,128)} async-done(((f32[4,27,4096]{2,1,0:T(8,128)}), f32[1,27,4096]{2,1,0:T(8,128)}) %reduce-scatter.5.cloned.1.call-update) | async-done | bytes 442384 | tf_op jit(solution)/shard_map/reduce_scatter | solution.py:87
  (190 shorter events, 198.7 us)
Async XLA Ops:
  6.5 66.3 %all-gather.2.cloned.1.call-start = ((), (), s32[]{:S(2)}) async-start(), calls=%async_computation.4 | async-start | bytes 3538944 | tf_op jit(solution)/shard_map/all_gather | solution.py:31
  7.3 731.7 %reduce-scatter.3.cloned.1.call-start = ((), (), s32[]{:S(2)}) async-start(), calls=%async_computation.5 | async-start | bytes 5242880 | tf_op jit(solution)/shard_map/reduce_scatter | solution.py:53
  17.0 11.9 %copy-start.3 = (s32[1,1,3,448]{3,1,2,0:T(1,128)S(1)}, s32[1,1,3,448]{3,1,2,0:T(1,128)}, u32[]{:S(2)}) copy-start(s32[1,1,3,448]{3,1,2,0:T(1,128)} %param.14) | copy-start | bytes 16132
  413.5 0.7 copy-start.2
  413.5 1.0 copy-start.1
  413.5 1.2 copy-start.4
  413.5 288.3 %copy-start = (f32[8,3,4096]{2,0,1:T(8,128)S(1)}, f32[8,3,4096]{2,0,1:T(8,128)}, u32[]{:S(2)}) copy-start(f32[8,3,4096]{2,0,1:T(8,128)} %param.16) | copy-start | bytes 1179652
  415.2 1.2 copy-start.5
  416.4 340.3 %all-to-all-start = ((f32[8,4,7]{2,1,0:T(4,128)}), f32[8,4,7]{2,1,0:T(4,128)S(1)}, u32[]{:S(2)}, u32[]{:S(2)}) async-start(f32[8,4,7]{2,1,0:T(4,128)} %bitcast.7), calls=%async_computation | async-start | bytes 32768 | tf_op jit(solution)/shard_map/all_to_all | solution.py:73
  747.5 2.5 copy-start.6
  756.7 98.8 %all-to-all-start.1 = ((f32[32,7,4096]{2,1,0:T(8,128)}), f32[32,7,4096]{2,1,0:T(8,128)}, u32[]{:S(2)}, u32[]{:S(2)}) async-start(f32[32,7,4096]{2,1,0:T(8,128)} %scatter_fusion.1), calls=%async_computation.2 | async-start | bytes 8388608 | tf_op jit(solution)/shard_map/all_to_all | solution.py:72
  762.3 172.5 %reduce-scatter.5.cloned.1.call-start = ((), (), s32[]{:S(2)}) async-start(), calls=%async_computation.6 | async-start | bytes 2621440 | tf_op jit(solution)/shard_map/reduce_scatter | solution.py:87
Sparse Core Ops, SparseCore 0:
  9.5 63.2 all-gather.1
  413.6 325.2 reduce-scatter.2
  905.2 29.5 reduce-scatter.4
where the time goes:
time: 951 us; the launch traced here: 944 us
  starting transfers between devices  291 us (31%)
  local copies, waits for them, and re-layouts  246 us (26%)
  waiting for transfers between devices  204 us (21%)
  matrix products  96 us (10%)
  other arithmetic  92.3 us (10%)
  between operations  13.9 us (1%)
    all_to_all x1, starting transfers between devices, on_device(): lax.all_to_all(meta_send, 'row', split_axis=0, concat_axis=0, tiled=True)  285 us
    all_to_all x1, waiting for transfers between devices, on_device(): lax.all_to_all(outgoing, 'row', split_axis=0, concat_axis=0, tiled=True)  92.8 us
    dot_general x15, matrix products, add_batch(): jnp.einsum('tij,tsjk->tsik', block_tiles, right_tiles, precision=highest)  82.8 us
    gather x15, local copies, waits for them, and re-layouts, add_batch(): right_tiles = jnp.take(panel_tiles, block_cols, axis=0)  69.3 us
    scatter-add x15, other arithmetic, add_batch(): partial_value.at[target.reshape(-1)]  50 us
    select_n x15, local copies, waits for them, and re-layouts, add_batch(): products = jnp.where(is_live[:, None, None, None], products, 0.0)  46 us
    all_gather x1, waiting for transfers between devices, on_device(): panel = lax.all_gather(p_vals, 'row', axis=0, tiled=True)  43.8 us
    reshape x15, local copies, waits for them, and re-layouts, add_batch(): products.reshape(tile_batch * branches, tile_len)  41.9 us
  transfers between devices with their start and end apart: 5, of which 4 were waited for; matrix products, arithmetic and copies ran while one was open for 4% of the time, Pallas kernels for 0%

commit v1 on v0

v1 whole, which is shorter than its diff:
```python
import functools

import jax
import jax.numpy as jnp
from jax import lax
from jax.experimental import pallas as pl
from jax.experimental.pallas import tpu as pltpu
from jax.sharding import PartitionSpec as P

BLOCK = 64
HALF = 32
LANES = 128
CPD = 1
TAP = 6
TC = 27
UNROLL = 4

VMEM = pl.BlockSpec(memory_space=pltpu.VMEM)
SMEM = pl.BlockSpec(memory_space=pltpu.SMEM)


def low_lanes(rows):
    return lax.broadcasted_iota(jnp.int32, (rows, LANES), 1) < BLOCK


def halves(value):
    high = value.astype(jnp.bfloat16)
    return high, (value - high.astype(jnp.float32)).astype(jnp.bfloat16)


def side_by_side(first, second):
    low = low_lanes(HALF)
    even = jnp.where(low, first, pltpu.roll(second, BLOCK, 1))
    odd = jnp.where(low, pltpu.roll(first, BLOCK, 1), second)
    return even, odd


def alone(first):
    low = low_lanes(HALF)
    return jnp.where(low, first, 0.0), jnp.where(low, pltpu.roll(first, BLOCK, 1), 0.0)


def ap_kernel(columns, targets, count_ref, col_ref, target_ref, a_ref, panel_ref, out_ref, weights, total, rows_ref):
    capacity = a_ref.shape[0]

    def weight_step(k, carry):
        first = panel_ref[3 * k]
        second = panel_ref[3 * k + 1]
        third = panel_ref[3 * k + 2]
        even, odd = side_by_side(first, second)
        rows_ref[0, pl.ds(0, HALF, stride=2), :] = even
        rows_ref[0, pl.ds(1, HALF, stride=2), :] = odd
        even, odd = alone(third)
        rows_ref[1, pl.ds(0, HALF, stride=2), :] = even
        rows_ref[1, pl.ds(1, HALF, stride=2), :] = odd
        high, rest = halves(jnp.concatenate([rows_ref[0], rows_ref[1]], axis=1))
        weights[k, 0:64, :] = high
        weights[k, 64:128, :] = high
        weights[k, 128:192, :] = rest
        weights[k, 192:256, :] = rest
        return carry

    lax.fori_loop(0, columns, weight_step, 0)

    def zero_step(i, carry):
        total[i] = jnp.zeros((BLOCK, LANES), jnp.float32)
        return carry

    lax.fori_loop(0, targets + 1, zero_step, 0)
    low_a = low_lanes(HALF)
    low = low_lanes(BLOCK)

    def block_step(step, carry):
        results = []
        for u in range(UNROLL):
            t = step * UNROLL + u
            value = a_ref[t]
            rounded = value.astype(jnp.bfloat16).astype(jnp.float32)
            rest = value - rounded
            even = jnp.where(low_a, rounded, pltpu.roll(rest, BLOCK, 1))
            odd = jnp.where(low_a, pltpu.roll(rounded, BLOCK, 1), rest)
            left = jnp.concatenate([even, odd], axis=0).astype(jnp.bfloat16)
            left = jnp.concatenate([left, left], axis=1)
            results.append(jnp.dot(left, weights[col_ref[t]], preferred_element_type=jnp.float32))
        for u in range(UNROLL):
            t = step * UNROLL + u
            pair = results[u][:, 0:LANES]
            total[target_ref[t]] += jnp.where(low, pair, 0.0)
            total[target_ref[capacity + t]] += jnp.where(low, 0.0, pair)
            total[target_ref[2 * capacity + t]] += results[u][:, LANES:2 * LANES]
        return carry

    lax.fori_loop(0, (count_ref[0] + UNROLL - 1) // UNROLL, block_step, 0)

    def out_step(i, carry):
        value = total[i]
        value = value + pltpu.roll(value, BLOCK, 1)
        out_ref[i] = jnp.where(low_a, value[0:HALF], value[HALF:BLOCK])
        return carry

    lax.fori_loop(0, targets, out_step, 0)


def coarse_kernel(rows, place_ref, ap_ref, p_ref, out_ref, result_ref):
    low = low_lanes(HALF)

    def row_step(i, carry):
        rights = []
        for pair in range(TAP // 2):
            even, odd = side_by_side(ap_ref[TAP * i + 2 * pair], ap_ref[TAP * i + 2 * pair + 1])
            rights.append(jnp.concatenate([even, odd], axis=0))
        high, rest = halves(jnp.concatenate(rights, axis=1))
        right = jnp.concatenate([high, rest, high, rest], axis=0)
        left_pair = jnp.concatenate(side_by_side(p_ref[3 * i], p_ref[3 * i + 1]), axis=0)
        left_one = jnp.concatenate(alone(p_ref[3 * i + 2]), axis=0)
        high, rest = halves(jnp.concatenate([left_pair, left_one], axis=1))
        left = jnp.concatenate([high, high, rest, rest], axis=0)
        result = lax.dot_general(
            left, right, (((0,), (0,)), ((), ())), preferred_element_type=jnp.float32
        )
        for pair in range(TAP // 2):
            result_ref[pair] = result[:, pair * LANES:(pair + 1) * LANES]
        for s in range(3):
            base = place_ref[3 * i + s] * TAP
            for pair in range(TAP // 2):
                even = result_ref[pair, pl.ds(s * BLOCK, HALF, stride=2), :]
                odd = result_ref[pair, pl.ds(s * BLOCK + 1, HALF, stride=2), :]
                out_ref[base + 2 * pair] = jnp.where(low, even, pltpu.roll(odd, BLOCK, 1))
                out_ref[base + 2 * pair + 1] = jnp.where(low, pltpu.roll(even, BLOCK, 1), odd)
        return carry

    lax.fori_loop(0, rows, row_step, 0)


def add_kernel(target_ref, in_ref, out_ref):
    out_ref[...] = jnp.zeros_like(out_ref)

    def step(e, carry):
        target = target_ref[e]

        @pl.when(target >= 0)
        def _():
            out_ref[target] += in_ref[e]

        return carry

    lax.fori_loop(0, in_ref.shape[0], step, 0)


def on_device(a_vals, a_row, a_col, a_slot, a_count, p_vals, p_owner, p_sub, ap_cslot):
    row_devices = lax.axis_size("row")
    col_devices = lax.axis_size("col")
    capacity = a_vals.shape[2]
    rows_dev = p_vals.shape[0]
    branches = p_vals.shape[1]
    group_rows = rows_dev * col_devices
    group_coarse = CPD * col_devices
    columns = rows_dev * row_devices
    targets = group_rows * TAP
    per_peer = max(2, 3 * rows_dev * branches // (2 * row_devices))
    item_count = rows_dev * branches
    slots_total = row_devices * per_peer
    f32 = jnp.float32

    p_local = p_vals.reshape(item_count, HALF, LANES)
    panel = lax.all_gather(p_local, "row", axis=0, tiled=True)

    a_blocks = a_vals.reshape(capacity, HALF, LANES)
    count = a_count.reshape(1)
    col_index = a_col.reshape(capacity)
    live = jnp.arange(capacity, dtype=jnp.int32) < count
    target = a_row.reshape(1, capacity) * TAP + a_slot.reshape(branches, capacity)
    target = jnp.where(live[None, :], target, targets).reshape(branches * capacity)

    owners = p_owner.reshape(item_count)
    serial = jnp.arange(item_count, dtype=jnp.int32)
    earlier = (owners[:, None] == owners[None, :]) & (serial[None, :] < serial[:, None])
    placed = owners * per_peer + jnp.sum(earlier.astype(jnp.int32), axis=1)
    metadata = p_sub.reshape(item_count, 1) * TC + ap_cslot.reshape(item_count, TAP)
    meta_send = jnp.full((slots_total, TAP), -1.0, f32).at[placed].set(metadata.astype(f32))
    meta_in = lax.all_to_all(meta_send, "row", split_axis=0, concat_axis=0, tiled=True)
    arrived_target = meta_in.astype(jnp.int32).reshape(slots_total * TAP)

    partial_ap = pl.pallas_call(
        functools.partial(ap_kernel, columns, targets),
        out_shape=jax.ShapeDtypeStruct((targets, HALF, LANES), f32),
        in_specs=[SMEM, SMEM, SMEM, VMEM, VMEM],
        out_specs=VMEM,
        scratch_shapes=[
            pltpu.VMEM((columns, 4 * BLOCK, 2 * LANES), jnp.bfloat16),
            pltpu.VMEM((targets + 1, BLOCK, LANES), f32),
            pltpu.VMEM((2, BLOCK, LANES), f32),
        ],
        compiler_params=pltpu.CompilerParams(vmem_limit_bytes=60 << 20),
        cost_estimate=pl.CostEstimate(
            flops=capacity * 2 * 64 * 256 * 256, bytes_accessed=14 << 20, transcendentals=0
        ),
        name="ap",
    )(count, col_index, target, a_blocks, panel)

    ap_rows = lax.psum_scatter(partial_ap, "col", scatter_dimension=0, tiled=True)

    outgoing = pl.pallas_call(
        functools.partial(coarse_kernel, rows_dev),
        out_shape=jax.ShapeDtypeStruct((slots_total * TAP, HALF, LANES), f32),
        in_specs=[SMEM, VMEM, VMEM],
        out_specs=VMEM,
        scratch_shapes=[pltpu.VMEM((TAP // 2, 2 * LANES, LANES), f32)],
        compiler_params=pltpu.CompilerParams(vmem_limit_bytes=32 << 20),
        name="coarse",
    )(placed, ap_rows, p_local)

    incoming = lax.all_to_all(outgoing, "row", split_axis=0, concat_axis=0, tiled=True)

    coarse_part = pl.pallas_call(
        add_kernel,
        out_shape=jax.ShapeDtypeStruct((group_coarse * TC, HALF, LANES), f32),
        in_specs=[SMEM, VMEM],
        out_specs=VMEM,
        compiler_params=pltpu.CompilerParams(vmem_limit_bytes=32 << 20),
        name="gather_coarse",
    )(arrived_target, incoming)

    coarse = lax.psum_scatter(coarse_part, "col", scatter_dimension=0, tiled=True)
    return coarse.reshape(CPD, TC, BLOCK * BLOCK)


def solution(mesh):
    placed = (
        P("row", "col", None, None),
        P("row", "col", None),
        P("row", "col", None),
        P("row", "col", None, None),
        P("row", "col"),
        P(("row", "col"), None, None),
        P(("row", "col"), None),
        P(("row", "col"), None),
        P(("row", "col"), None, None),
    )
    return jax.shard_map(
        on_device,
        mesh=mesh,
        in_specs=placed,
        out_specs=P(("row", "col"), None, None),
        check_vma=False,
    )
```

time: 951 us -> 290 us (0.30)
  starting transfers between devices: 291 us -> 9.03 us
  local copies, waits for them, and re-layouts: 246 us -> 15.3 us
  matrix products: 96 us -> 0 us
  other arithmetic: 92.3 us -> 2.22 us
  Pallas kernels: 0 us -> 67.9 us
  waiting for transfers between devices: 204 us -> 181 us
    all_to_all x1, starting transfers between devices: 285 us -> 3.42 us  [on_device(): lax.all_to_all(meta_send, 'row', split_axis=0, concat_axis=0, tiled=True)]
    dot_general x16 -> x0, matrix products: 96 us -> none  [the longest x15 82.8 us: add_batch(): jnp.einsum('tij,tsjk->tsik', block_tiles, right_tiles, precision=highest)]
    gather x15 -> x0, local copies, waits for them, and re-layouts: 69.3 us -> none  [add_batch(): right_tiles = jnp.take(panel_tiles, block_cols, axis=0)]
    pallas_call x0 -> x3, Pallas kernels: none -> 67.9 us  [the longest x1 59 us: on_device(): pl.pallas_call(functools.partial(ap_kernel, columns, targets), out_shape=...]
    reshape x38 -> x2, local copies, waits for them, and re-layouts: 62.8 us -> 1.12 us  [the longest x1 1.04 us: on_device(): p_local = p_vals.reshape(item_count, HALF, LANES)]
    scatter-add x16 -> x0, other arithmetic: 56.3 us -> none  [the longest x15 50 us: add_batch(): partial_value.at[target.reshape(-1)]]
    select_n x15 -> x0, local copies, waits for them, and re-layouts: 46 us -> none  [add_batch(): products = jnp.where(is_live[:, None, None, None], products, 0.0)]
    all_to_all x1, waiting for transfers between devices: 92.8 us -> 70.5 us  [on_device(): lax.all_to_all(outgoing, 'row', split_axis=0, concat_axis=0, tiled=True)]
  transfers between devices with their start and end apart: 5 -> 5, of which waited for: 4 -> 4; matrix products, arithmetic and copies ran while one was open for 4% -> 4% of each run, Pallas kernels for 0% -> 2%
where the time goes in v1:
time: 290 us; the launch traced here: 289 us
  waiting for transfers between devices  181 us (62%)
  Pallas kernels  67.9 us (23%)
  local copies, waits for them, and re-layouts  15.3 us (5%)
  between operations  13.8 us (5%)
  starting transfers between devices  9.03 us (3%)
    all_to_all x1, waiting for transfers between devices, on_device(): lax.all_to_all(outgoing, 'row', split_axis=0, concat_axis=0, tiled=True)  70.5 us
    pallas_call x1, Pallas kernels, on_device(): pl.pallas_call(functools.partial(ap_kernel, columns, targets), out_shape=...  59 us
    all_gather x1, waiting for transfers between devices, on_device(): panel = lax.all_gather(p_local, 'row', axis=0, tiled=True)  53.3 us
    reduce_scatter x1, waiting for transfers between devices, on_device(): lax.psum_scatter(partial_ap, 'col', scatter_dimension=0, tiled=True)  29.8 us
    reduce_scatter x1, waiting for transfers between devices, on_device(): lax.psum_scatter(coarse_part, 'col', scatter_dimension=0, tiled=True)  27.6 us
    unnamed x16, local copies, waits for them, and re-layouts  12.1 us
  transfers between devices with their start and end apart: 5, of which 4 were waited for; matrix products, arithmetic and copies ran while one was open for 4% of the time, Pallas kernels for 2%

profile of v1, /device:TPU:0, one launch (start us, length us, event | category | flops | bytes accessed | tf_op | source)
XLA Modules:
  0.0 289.5 jit_solution(18065868264388220481)
XLA Ops:
  6.5 0.0 all-gather.2.cloned.1.call-start
  6.5 1.3 copy.40
  7.8 1.0 reshape.91.p_ref
  8.8 0.0 all-gather.2.cloned.1.call-update
  8.9 0.0 reduce-scatter.3.cloned.1.call-start
  9.6 0.1 broadcast_in_dim.23
  9.7 0.7 broadcast_multiply_fusion
  10.4 0.1 add.44
  10.5 0.7 reduce
  11.2 0.1 reshape.89
  11.3 7.6 %copy.42 = f32[56,8,32,128]{3,2,1,0:T(8,128)} copy(f32[56,8,32,128]{3,1,2,0:T(8,128)} %bitcast.20) | data formatting | bytes 14680064
  18.9 0.6 add_select_fusion.target_ref
  19.5 53.3 %all-gather.2.cloned.1.call-done.panel_ref = f32[192,32,128]{2,1,0:T(8,128)} async-done(((f32[24,32,128]{2,1,0:T(8,128)}), f32[192,32,128]{2,1,0:T(8,128)}) %all-gather.2.cloned.1.call-update) | async-done | bytes 3145744 | tf_op jit(solution)/shard_map/all_gather | solution.py:166
  72.7 59.0 %ap.1 = f32[192,32,128]{2,1,0:T(8,128)} custom-call(s32[1]{0:T(128)} %bitcast.18.count_ref, s32[448]{0:T(512)} %bitcast.23, s32[1344]{0:T(1024)} %add_select_fusion.target_ref, f32[448,32,128]{2,1,0:T(8,128)} %bitcast.21, f32[192,32,128]{2,1,0:T(8,128)} %all-gather.2.cloned.1.call-done.panel_ref), custom_call_target="tpu_custom_call" | custom-call | flops 3758096384 | bytes 14680064 | tf_op jit(solution)/shard_map/ap/pallas_call | solution.py:184
  131.7 0.0 copy-start.4
  131.7 0.0 copy-start.3
  131.7 0.0 copy-start.5
  131.7 0.0 copy-start.1
  131.7 0.0 reduce-scatter.3.cloned.1.call-update
  131.7 0.6 copy-done.4
  132.4 0.1 copy.36
  132.5 0.1 eq.15
  132.5 0.1 copy.35
  132.6 0.1 mul.41
  132.7 0.0 copy-done.3
  132.7 0.1 copy.38
  132.8 0.1 reshape.86
  132.9 0.0 copy-done.5
  132.9 0.1 copy.37
  133.0 0.1 mul.43
  133.1 0.1 copy.39
  133.2 0.2 convert_reduce_fusion
  133.4 1.2 scatter_custom_fusion
  134.6 3.4 %all-to-all-start = ((f32[8,4,6]{2,1,0:T(4,128)}), f32[8,4,6]{2,1,0:T(4,128)S(1)}, u32[]{:S(2)}, u32[]{:S(2)}) async-start(f32[8,4,6]{2,1,0:T(4,128)} %bitcast.2), calls=%async_computation | async-start | bytes 32768 | tf_op jit(solution)/shard_map/all_to_all | solution.py:181
  138.0 29.8 %reduce-scatter.3.cloned.1.call-done.ap_ref = f32[48,32,128]{2,1,0:T(8,128)} async-done(((f32[192,32,128]{2,1,0:T(8,128)}), f32[48,32,128]{2,1,0:T(8,128)}) %reduce-scatter.3.cloned.1.call-update) | async-done | bytes 786448 | tf_op jit(solution)/shard_map/reduce_scatter | solution.py:201
  167.8 0.0 copy-done.1
  167.8 1.1 copy-done.2
  168.9 5.6 %coarse.1 = f32[192,32,128]{2,1,0:T(8,128)} custom-call(s32[24]{0:T(128)S(1)} %multiply_add_fusion.place_ref, f32[48,32,128]{2,1,0:T(8,128)S(1)} %copy-done.2, f32[24,32,128]{2,1,0:T(8,128)S(1)} %copy-done.1), custom_call_target="tpu_custom_call" | custom-call | tf_op jit(solution)/shard_map/coarse/pallas_call | solution.py:203
  174.5 0.0 all-to-all-done
  174.5 5.5 %all-to-all-start.1 = ((f32[192,32,128]{2,1,0:T(8,128)}), f32[192,32,128]{2,1,0:T(8,128)S(1)}, u32[]{:S(2)}, u32[]{:S(2)}) async-start(f32[192,32,128]{2,1,0:T(8,128)} %coarse.1), calls=%async_computation.2 | async-start | bytes 6291456 | tf_op jit(solution)/shard_map/all_to_all | solution.py:213
  180.0 0.0 reduce-scatter.5.cloned.1.call-start
  180.1 0.1 convert_element_type.16.target_ref
  180.2 70.5 %all-to-all-done.1.in_ref = f32[192,32,128]{2,1,0:T(8,128)S(1)} async-done(((f32[192,32,128]{2,1,0:T(8,128)}), f32[192,32,128]{2,1,0:T(8,128)S(1)}, u32[]{:S(2)}, u32[]{:S(2)}) %all-to-all-start.1) | async-done | bytes 3145760 | tf_op jit(solution)/shard_map/all_to_all | solution.py:213
  250.7 3.4 %gather_coarse.1 = f32[108,32,128]{2,1,0:T(8,128)S(1)} custom-call(s32[192]{0:T(256)S(1)} %convert_element_type.16.target_ref, f32[192,32,128]{2,1,0:T(8,128)S(1)} %all-to-all-done.1.in_ref), custom_call_target="tpu_custom_call" | custom-call | tf_op jit(solution)/shard_map/gather_coarse/pallas_call | solution.py:215
  254.1 0.0 copy-start
  254.1 1.2 copy-done
  255.3 0.0 reduce-scatter.5.cloned.1.call-update
  255.3 27.6 %reduce-scatter.5.cloned.1.call-done = f32[27,32,128]{2,1,0:T(8,128)} async-done(((f32[108,32,128]{2,1,0:T(8,128)}), f32[27,32,128]{2,1,0:T(8,128)}) %reduce-scatter.5.cloned.1.call-update) | async-done | bytes 442384 | tf_op jit(solution)/shard_map/reduce_scatter | solution.py:224
  (10 shorter events, 0.1 us)
Async XLA Ops:
  6.5 66.2 %all-gather.2.cloned.1.call-start = ((), (), s32[]{:S(2)}) async-start(), calls=%async_computation.4 | async-start | bytes 3538944 | tf_op jit(solution)/shard_map/all_gather | solution.py:166
  8.9 158.9 %reduce-scatter.3.cloned.1.call-start = ((), (), s32[]{:S(2)}) async-start(), calls=%async_computation.5 | async-start | bytes 3932160 | tf_op jit(solution)/shard_map/reduce_scatter | solution.py:201
  131.7 0.7 copy-start.4
  131.7 1.0 copy-start.3
  131.7 1.2 copy-start.5
  131.7 36.1 %copy-start.1 = (f32[24,32,128]{2,1,0:T(8,128)S(1)}, f32[24,32,128]{2,1,0:T(8,128)}, u32[]{:S(2)}) copy-start(f32[24,32,128]{2,1,0:T(8,128)} %reshape.91.p_ref) | copy-start | bytes 1179652
  134.6 39.9 %all-to-all-start = ((f32[8,4,6]{2,1,0:T(4,128)}), f32[8,4,6]{2,1,0:T(4,128)S(1)}, u32[]{:S(2)}, u32[]{:S(2)}) async-start(f32[8,4,6]{2,1,0:T(4,128)} %bitcast.2), calls=%async_computation | async-start | bytes 32768 | tf_op jit(solution)/shard_map/all_to_all | solution.py:181
  167.8 1.1 copy-start.2
  174.5 76.2 %all-to-all-start.1 = ((f32[192,32,128]{2,1,0:T(8,128)}), f32[192,32,128]{2,1,0:T(8,128)S(1)}, u32[]{:S(2)}, u32[]{:S(2)}) async-start(f32[192,32,128]{2,1,0:T(8,128)} %coarse.1), calls=%async_computation.2 | async-start | bytes 6291456 | tf_op jit(solution)/shard_map/all_to_all | solution.py:213
  180.0 102.9 %reduce-scatter.5.cloned.1.call-start = ((), (), s32[]{:S(2)}) async-start(), calls=%async_computation.6 | async-start | bytes 2211840 | tf_op jit(solution)/shard_map/reduce_scatter | solution.py:224
  254.1 1.2 copy-start
Sparse Core Ops, SparseCore 0:
  9.5 63.1 all-gather.1
  131.9 35.8 reduce-scatter.2
  255.5 27.4 reduce-scatter.4

commit v2 on v1

--- a/solution.py
+++ b/solution.py
@@ -13,7 +13,7 @@
 CPD = 1
 TAP = 6
 TC = 27
-UNROLL = 4
+CHUNK = 4
 
 VMEM = pl.BlockSpec(memory_space=pltpu.VMEM)
 SMEM = pl.BlockSpec(memory_space=pltpu.SMEM)
@@ -40,8 +40,67 @@
     return jnp.where(low, first, 0.0), jnp.where(low, pltpu.roll(first, BLOCK, 1), 0.0)
 
 
-def ap_kernel(columns, targets, count_ref, col_ref, target_ref, a_ref, panel_ref, out_ref, weights, total, rows_ref):
-    capacity = a_ref.shape[0]
+def plan_kernel(columns, dump, count_ref, col_ref, target_ref, order_ref, place_ref, chunk_ref, total_ref, fill):
+    capacity = col_ref.shape[0]
+    slots = order_ref.shape[0]
+    count = count_ref[0]
+
+    def clear_column(k, carry):
+        fill[k] = 0
+        return carry
+
+    lax.fori_loop(0, columns, clear_column, 0)
+
+    def clear_slot(i, carry):
+        order_ref[i] = 0
+        for s in range(3):
+            place_ref[s * (slots + CHUNK) + i] = dump
+        return carry
+
+    lax.fori_loop(0, slots, clear_slot, 0)
+    for i in range(CHUNK):
+        for s in range(3):
+            place_ref[s * (slots + CHUNK) + slots + i] = dump
+
+    def clear_chunk(i, carry):
+        chunk_ref[i] = 0
+        return carry
+
+    lax.fori_loop(0, slots // CHUNK, clear_chunk, 0)
+
+    def tally(t, carry):
+        fill[col_ref[t]] += 1
+        return carry
+
+    lax.fori_loop(0, count, tally, 0)
+
+    def open_column(k, first):
+        chunks = (fill[k] + CHUNK - 1) // CHUNK
+        fill[k] = first * CHUNK
+
+        def mark(j, carry):
+            chunk_ref[first + j] = k
+            return carry
+
+        lax.fori_loop(0, chunks, mark, 0)
+        return first + chunks
+
+    total_ref[0] = lax.fori_loop(0, columns, open_column, 0)
+
+    def put(t, carry):
+        k = col_ref[t]
+        at = fill[k]
+        fill[k] = at + 1
+        order_ref[at] = t
+        for s in range(3):
+            place_ref[s * (slots + CHUNK) + CHUNK + at] = target_ref[s * capacity + t]
+        return carry
+
+    lax.fori_loop(0, count, put, 0)
+
+
+def ap_kernel(columns, targets, chunks_ref, order_ref, place_ref, chunk_ref, a_ref, panel_ref, out_ref, weights, total, rows_ref, first_ref, second_ref):
+    slots = order_ref.shape[0]
 
     def weight_step(k, carry):
         first = panel_ref[3 * k]
@@ -70,27 +129,40 @@
     low_a = low_lanes(HALF)
     low = low_lanes(BLOCK)
 
-    def block_step(step, carry):
-        results = []
-        for u in range(UNROLL):
-            t = step * UNROLL + u
-            value = a_ref[t]
+    def multiply(c, result_ref):
+        parts = []
+        for u in range(CHUNK):
+            value = a_ref[order_ref[c * CHUNK + u]]
             rounded = value.astype(jnp.bfloat16).astype(jnp.float32)
             rest = value - rounded
             even = jnp.where(low_a, rounded, pltpu.roll(rest, BLOCK, 1))
             odd = jnp.where(low_a, pltpu.roll(rounded, BLOCK, 1), rest)
-            left = jnp.concatenate([even, odd], axis=0).astype(jnp.bfloat16)
-            left = jnp.concatenate([left, left], axis=1)
-            results.append(jnp.dot(left, weights[col_ref[t]], preferred_element_type=jnp.float32))
-        for u in range(UNROLL):
-            t = step * UNROLL + u
-            pair = results[u][:, 0:LANES]
-            total[target_ref[t]] += jnp.where(low, pair, 0.0)
-            total[target_ref[capacity + t]] += jnp.where(low, 0.0, pair)
-            total[target_ref[2 * capacity + t]] += results[u][:, LANES:2 * LANES]
-        return carry
-
-    lax.fori_loop(0, (count_ref[0] + UNROLL - 1) // UNROLL, block_step, 0)
+            parts += [even.astype(jnp.bfloat16), odd.astype(jnp.bfloat16)]
+        left = jnp.concatenate(parts, axis=0)
+        left = jnp.concatenate([left, left], axis=1)
+        result_ref[...] = jnp.dot(left, weights[chunk_ref[c]], preferred_element_type=jnp.float32)
+
+    def add(c, result_ref):
+        for u in range(CHUNK):
+            at = (c + 1) * CHUNK + u
+            rows = slice(u * BLOCK, (u + 1) * BLOCK)
+            pair = result_ref[rows, 0:LANES]
+            total[place_ref[at]] += jnp.where(low, pair, 0.0)
+            total[place_ref[slots + CHUNK + at]] += jnp.where(low, 0.0, pair)
+            total[place_ref[2 * (slots + CHUNK) + at]] += result_ref[rows, LANES:2 * LANES]
+
+    second_ref[...] = jnp.zeros_like(second_ref)
+    steps = (chunks_ref[0] + 1) // 2
+
+    def chunk_step(step, carry):
+        multiply(2 * step, first_ref)
+        add(2 * step - 1, second_ref)
+        multiply(2 * step + 1, second_ref)
+        add(2 * step, first_ref)
+        return carry
+
+    lax.fori_loop(0, steps, chunk_step, 0)
+    add(2 * steps - 1, second_ref)
 
     def out_step(i, carry):
         value = total[i]
@@ -168,9 +240,24 @@
     a_blocks = a_vals.reshape(capacity, HALF, LANES)
     count = a_count.reshape(1)
     col_index = a_col.reshape(capacity)
-    live = jnp.arange(capacity, dtype=jnp.int32) < count
-    target = a_row.reshape(1, capacity) * TAP + a_slot.reshape(branches, capacity)
-    target = jnp.where(live[None, :], target, targets).reshape(branches * capacity)
+    target = (a_row.reshape(1, capacity) * TAP + a_slot.reshape(branches, capacity)).reshape(branches * capacity)
+    chunk_cap = min(capacity, columns + capacity // CHUNK) + 2
+    slots = chunk_cap * CHUNK
+    i32 = jnp.int32
+    order, places, chunk_column, chunk_count = pl.pallas_call(
+        functools.partial(plan_kernel, columns, targets),
+        out_shape=(
+            jax.ShapeDtypeStruct((slots,), i32),
+            jax.ShapeDtypeStruct((branches * (slots + CHUNK),), i32),
+            jax.ShapeDtypeStruct((chunk_cap,), i32),
+            jax.ShapeDtypeStruct((1,), i32),
+        ),
+        in_specs=[SMEM, SMEM, SMEM],
+        out_specs=(SMEM, SMEM, SMEM, SMEM),
+        scratch_shapes=[pltpu.SMEM((columns,), i32)],
+        cost_estimate=pl.CostEstimate(flops=0, bytes_accessed=20 << 20, transcendentals=0),
+        name="plan",
+    )(count, col_index, target)
 
     owners = p_owner.reshape(item_count)
     serial = jnp.arange(item_count, dtype=jnp.int32)
@@ -181,22 +268,25 @@
     meta_in = lax.all_to_all(meta_send, "row", split_axis=0, concat_axis=0, tiled=True)
     arrived_target = meta_in.astype(jnp.int32).reshape(slots_total * TAP)
 
+    arrived_target, chunk_count = lax.optimization_barrier((arrived_target, chunk_count))
     partial_ap = pl.pallas_call(
         functools.partial(ap_kernel, columns, targets),
         out_shape=jax.ShapeDtypeStruct((targets, HALF, LANES), f32),
-        in_specs=[SMEM, SMEM, SMEM, VMEM, VMEM],
+        in_specs=[SMEM, SMEM, SMEM, SMEM, VMEM, VMEM],
         out_specs=VMEM,
         scratch_shapes=[
             pltpu.VMEM((columns, 4 * BLOCK, 2 * LANES), jnp.bfloat16),
             pltpu.VMEM((targets + 1, BLOCK, LANES), f32),
             pltpu.VMEM((2, BLOCK, LANES), f32),
+            pltpu.VMEM((CHUNK * BLOCK, 2 * LANES), f32),
+            pltpu.VMEM((CHUNK * BLOCK, 2 * LANES), f32),
         ],
         compiler_params=pltpu.CompilerParams(vmem_limit_bytes=60 << 20),
         cost_estimate=pl.CostEstimate(
             flops=capacity * 2 * 64 * 256 * 256, bytes_accessed=14 << 20, transcendentals=0
         ),
         name="ap",
-    )(count, col_index, target, a_blocks, panel)
+    )(chunk_count, order, places, chunk_column, a_blocks, panel)
 
     ap_rows = lax.psum_scatter(partial_ap, "col", scatter_dimension=0, tiled=True)
 

time: 290 us -> 279 us (0.962)
  waiting for transfers between devices: 181 us -> 86.6 us
  blocking collectives: 0 us -> 76 us
  Pallas kernels: 67.9 us -> 76.8 us
    all_to_all x0 -> x1, blocking collectives: none -> 76 us  [on_device(): lax.all_to_all(outgoing, 'row', split_axis=0, concat_axis=0, tiled=True)]
    all_to_all x1 -> x0, waiting for transfers between devices: 70.5 us -> none  [on_device(): lax.all_to_all(outgoing, 'row', split_axis=0, concat_axis=0, tiled=True)]
    all_gather x1, waiting for transfers between devices: 53.3 us -> 21.4 us  [on_device(): panel = lax.all_gather(p_local, 'row', axis=0, tiled=True)]
    pallas_call x0 -> x1, Pallas kernels: none -> 19.8 us  [on_device(): pl.pallas_call(functools.partial(plan_kernel, columns, targets), out_shap...]
    pallas_call x1, Pallas kernels: 59 us -> 48.4 us  [on_device(): pl.pallas_call(functools.partial(ap_kernel, columns, targets), out_shape=...]
    reduce_scatter x1, waiting for transfers between devices: 29.8 us -> 37.6 us  [on_device(): lax.psum_scatter(partial_ap, 'col', scatter_dimension=0, tiled=True)]
    all_to_all x1 -> x0, starting transfers between devices: 5.53 us -> none  [on_device(): lax.all_to_all(outgoing, 'row', split_axis=0, concat_axis=0, tiled=True)]
    all_to_all x1, starting transfers between devices: 3.42 us -> 7.25 us  [on_device(): lax.all_to_all(meta_send, 'row', split_axis=0, concat_axis=0, tiled=True)]
  transfers between devices with their start and end apart: 5 -> 4, of which waited for: 4 -> 3; matrix products, arithmetic and copies ran while one was open for 4% -> 5% of each run, Pallas kernels for 2% -> 7%
where the time goes in v2:
time: 279 us
  waiting for transfers between devices  86.6 us (31%)
  Pallas kernels  76.8 us (28%)
  blocking collectives  76 us (27%)
  local copies, waits for them, and re-layouts  14.7 us (5%)
  between operations  13.8 us (5%)
  starting transfers between devices  7.33 us (3%)
  other arithmetic  3.57 us (1%)
    all_to_all x1, blocking collectives, on_device(): lax.all_to_all(outgoing, 'row', split_axis=0, concat_axis=0, tiled=True)  76 us
    pallas_call x1, Pallas kernels, on_device(): pl.pallas_call(functools.partial(ap_kernel, columns, targets), out_shape=...  48.4 us
    reduce_scatter x1, waiting for transfers between devices, on_device(): lax.psum_scatter(partial_ap, 'col', scatter_dimension=0, tiled=True)  37.6 us
    reduce_scatter x1, waiting for transfers between devices, on_device(): lax.psum_scatter(coarse_part, 'col', scatter_dimension=0, tiled=True)  27.6 us
    all_gather x1, waiting for transfers between devices, on_device(): panel = lax.all_gather(p_local, 'row', axis=0, tiled=True)  21.4 us
    pallas_call x1, Pallas kernels, on_device(): pl.pallas_call(functools.partial(plan_kernel, columns, targets), out_shap...  19.8 us
    unnamed x8, local copies, waits for them, and re-layouts  11.6 us
    all_to_all x1, starting transfers between devices, on_device(): lax.all_to_all(meta_send, 'row', split_axis=0, concat_axis=0, tiled=True)  7.25 us
  transfers between devices with their start and end apart: 4, of which 3 were waited for; matrix products, arithmetic and copies ran while one was open for 5% of the time, Pallas kernels for 7%

profile of v2, /device:TPU:0, one launch (start us, length us, event | category | flops | bytes accessed | tf_op | source)
XLA Modules:
  0.0 278.9 jit_solution(13225109875930488259)
XLA Ops:
  6.5 0.0 all-gather.2.cloned.1.call-start
  6.5 1.3 copy.40
  7.8 1.0 reshape.85.p_ref
  8.8 0.0 all-gather.2.cloned.1.call-update
  8.9 0.7 broadcast_multiply_fusion.1
  9.6 0.1 copy.37
  9.6 0.1 mul.43
  9.7 0.8 copy.36
  10.5 0.7 broadcast_multiply_fusion.2
  11.2 0.1 copy.35
  11.3 0.1 mul.41
  11.3 0.1 eq.15
  11.4 0.8 copy.38
  12.3 0.1 reshape.80
  12.3 0.1 copy.39
  12.4 0.2 convert_reduce_fusion
  12.6 1.2 scatter_custom_fusion
  13.8 7.3 %all-to-all-start = ((f32[8,4,6]{2,1,0:T(4,128)}), f32[8,4,6]{2,1,0:T(4,128)S(1)}, u32[]{:S(2)}, u32[]{:S(2)}) async-start(f32[8,4,6]{2,1,0:T(4,128)} %bitcast.2), calls=%async_computation | async-start | bytes 32768 | tf_op jit(solution)/shard_map/all_to_all | solution.py:268
  21.1 0.0 reduce-scatter.3.cloned.1.call-start
  21.1 0.7 broadcast_multiply_fusion
  22.5 0.1 add.43
  22.6 0.7 reduce
  23.3 0.1 reshape.83
  23.4 7.6 %copy.42 = f32[56,8,32,128]{3,2,1,0:T(8,128)} copy(f32[56,8,32,128]{3,1,2,0:T(8,128)} %bitcast.19) | data formatting | bytes 14680064
  31.0 0.6 add.44.target_ref
  31.6 19.8 %plan.1 = (s32[712]{0:T(1024)}, s32[2148]{0:T(1024)}, s32[178]{0:T(256)}, s32[1]{0:T(128)}) custom-call(s32[1]{0:T(128)} %bitcast.17.count_ref, s32[448]{0:T(512)} %bitcast.22, s32[1344]{0:T(1024)} %add.44.target_ref), custom_call_target="tpu_custom_call" | custom-call | bytes 20971520 | tf_op jit(solution)/shard_map/plan/pallas_call | solution.py:247
  51.4 0.0 all-to-all-done
  51.4 0.1 convert_element_type.16.target_ref
  51.5 21.4 %all-gather.2.cloned.1.call-done.panel_ref = f32[192,32,128]{2,1,0:T(8,128)} async-done(((f32[24,32,128]{2,1,0:T(8,128)}), f32[192,32,128]{2,1,0:T(8,128)}) %all-gather.2.cloned.1.call-update) | async-done | bytes 3145744 | tf_op jit(solution)/shard_map/all_gather | solution.py:238
  72.9 48.4 %ap.1 = f32[192,32,128]{2,1,0:T(8,128)} custom-call(s32[1]{0:T(128)} %get-tuple-element.13.chunks_ref, s32[712]{0:T(1024)} %get-tuple-element.14.order_ref, s32[2148]{0:T(1024)} %get-tuple-element.15.place_ref, s32[178]{0:T(256)} %get-tuple-element.16.chunk_ref, f32[448,32,128]{2,1,0:T(8,128)} %bitcast.20, f32[192,32,128]{2,1,0:T(8,128)} %all-gather.2.cloned.1.call-done.panel_ref), custom_call_target="tpu_custom_call" | custom-call | flops 3758096384 | bytes 14680064 | tf_op jit(solution)/shard_map/ap/pallas_call | solution.py:272
  121.3 0.0 copy-start
  121.3 0.0 reduce-scatter.3.cloned.1.call-update
  121.3 0.0 reduce-scatter.5.cloned.1.call-start
  121.4 37.6 %reduce-scatter.3.cloned.1.call-done.ap_ref = f32[48,32,128]{2,1,0:T(8,128)} async-done(((f32[192,32,128]{2,1,0:T(8,128)}), f32[48,32,128]{2,1,0:T(8,128)}) %reduce-scatter.3.cloned.1.call-update) | async-done | bytes 786448 | tf_op jit(solution)/shard_map/reduce_scatter | solution.py:291
  159.0 0.0 copy-done
  159.0 0.0 copy-start.1
  159.0 1.1 copy-done.1
  160.1 3.9 %coarse.1 = f32[192,32,128]{2,1,0:T(8,128)S(1)} custom-call(s32[24]{0:T(128)S(1)} %multiply_add_fusion.place_ref, f32[48,32,128]{2,1,0:T(8,128)S(1)} %copy-done.1, f32[24,32,128]{2,1,0:T(8,128)S(1)} %copy-done), custom_call_target="tpu_custom_call" | custom-call | tf_op jit(solution)/shard_map/coarse/pallas_call | solution.py:293
  164.1 76.0 %all_to_all.14.in_ref = f32[192,32,128]{2,1,0:T(8,128)S(1)} all-to-all(f32[192,32,128]{2,1,0:T(8,128)S(1)} %coarse.1), channel_id=1, replica_groups=mesh['row'=8,'col'=4] {'row'}, dimensions={0} | all-to-all | bytes 6291456 | tf_op jit(solution)/shard_map/all_to_all | solution.py:303
  240.1 4.7 %gather_coarse.1 = f32[108,32,128]{2,1,0:T(8,128)} custom-call(s32[192]{0:T(256)S(1)} %convert_element_type.16.target_ref, f32[192,32,128]{2,1,0:T(8,128)S(1)} %all_to_all.14.in_ref), custom_call_target="tpu_custom_call" | custom-call | tf_op jit(solution)/shard_map/gather_coarse/pallas_call | solution.py:305
  244.8 0.0 reduce-scatter.5.cloned.1.call-update
  244.8 27.6 %reduce-scatter.5.cloned.1.call-done = f32[27,32,128]{2,1,0:T(8,128)} async-done(((f32[108,32,128]{2,1,0:T(8,128)}), f32[27,32,128]{2,1,0:T(8,128)}) %reduce-scatter.5.cloned.1.call-update) | async-done | bytes 442384 | tf_op jit(solution)/shard_map/reduce_scatter | solution.py:314
  (5 shorter events, 0.0 us)
Async XLA Ops:
  6.5 66.3 %all-gather.2.cloned.1.call-start = ((), (), s32[]{:S(2)}) async-start(), calls=%async_computation.4 | async-start | bytes 3538944 | tf_op jit(solution)/shard_map/all_gather | solution.py:238
  13.8 37.6 %all-to-all-start = ((f32[8,4,6]{2,1,0:T(4,128)}), f32[8,4,6]{2,1,0:T(4,128)S(1)}, u32[]{:S(2)}, u32[]{:S(2)}) async-start(f32[8,4,6]{2,1,0:T(4,128)} %bitcast.2), calls=%async_computation | async-start | bytes 32768 | tf_op jit(solution)/shard_map/all_to_all | solution.py:268
  21.1 137.9 %reduce-scatter.3.cloned.1.call-start = ((), (), s32[]{:S(2)}) async-start(), calls=%async_computation.5 | async-start | bytes 3932160 | tf_op jit(solution)/shard_map/reduce_scatter | solution.py:291
  121.3 37.7 %copy-start = (f32[24,32,128]{2,1,0:T(8,128)S(1)}, f32[24,32,128]{2,1,0:T(8,128)}, u32[]{:S(2)}) copy-start(f32[24,32,128]{2,1,0:T(8,128)} %reshape.85.p_ref) | copy-start | bytes 1179652
  121.3 151.1 %reduce-scatter.5.cloned.1.call-start = ((), (), s32[]{:S(2)}) async-start(), calls=%async_computation.6 | async-start | bytes 2211840 | tf_op jit(solution)/shard_map/reduce_scatter | solution.py:314
  159.0 1.1 copy-start.1
Sparse Core Ops, SparseCore 0:
  9.5 63.2 all-gather.1
  121.4 37.5 reduce-scatter.2
  244.9 27.4 reduce-scatter.4

commit v3 on v2

--- a/solution.py
+++ b/solution.py
@@ -14,6 +14,8 @@
 TAP = 6
 TC = 27
 CHUNK = 4
+WEIGHTS = 4
+OUTS = 6
 
 VMEM = pl.BlockSpec(memory_space=pltpu.VMEM)
 SMEM = pl.BlockSpec(memory_space=pltpu.SMEM)
@@ -102,30 +104,34 @@
 def ap_kernel(columns, targets, chunks_ref, order_ref, place_ref, chunk_ref, a_ref, panel_ref, out_ref, weights, total, rows_ref, first_ref, second_ref):
     slots = order_ref.shape[0]
 
-    def weight_step(k, carry):
-        first = panel_ref[3 * k]
-        second = panel_ref[3 * k + 1]
-        third = panel_ref[3 * k + 2]
-        even, odd = side_by_side(first, second)
-        rows_ref[0, pl.ds(0, HALF, stride=2), :] = even
-        rows_ref[0, pl.ds(1, HALF, stride=2), :] = odd
-        even, odd = alone(third)
-        rows_ref[1, pl.ds(0, HALF, stride=2), :] = even
-        rows_ref[1, pl.ds(1, HALF, stride=2), :] = odd
-        high, rest = halves(jnp.concatenate([rows_ref[0], rows_ref[1]], axis=1))
-        weights[k, 0:64, :] = high
-        weights[k, 64:128, :] = high
-        weights[k, 128:192, :] = rest
-        weights[k, 192:256, :] = rest
-        return carry
-
-    lax.fori_loop(0, columns, weight_step, 0)
-
-    def zero_step(i, carry):
-        total[i] = jnp.zeros((BLOCK, LANES), jnp.float32)
-        return carry
-
-    lax.fori_loop(0, targets + 1, zero_step, 0)
+    def weight_step(step, carry):
+        for j in range(WEIGHTS):
+            k = step * WEIGHTS + j
+            even, odd = side_by_side(panel_ref[3 * k], panel_ref[3 * k + 1])
+            rows_ref[j, 0, pl.ds(0, HALF, stride=2), :] = even
+            rows_ref[j, 0, pl.ds(1, HALF, stride=2), :] = odd
+            even, odd = alone(panel_ref[3 * k + 2])
+            rows_ref[j, 1, pl.ds(0, HALF, stride=2), :] = even
+            rows_ref[j, 1, pl.ds(1, HALF, stride=2), :] = odd
+        for j in range(WEIGHTS):
+            k = step * WEIGHTS + j
+            for side in range(2):
+                lanes = slice(side * LANES, (side + 1) * LANES)
+                high, rest = halves(rows_ref[j, side])
+                weights[k, 0:64, lanes] = high
+                weights[k, 64:128, lanes] = high
+                weights[k, 128:192, lanes] = rest
+                weights[k, 192:256, lanes] = rest
+        return carry
+
+    lax.fori_loop(0, columns // WEIGHTS, weight_step, 0)
+
+    def zero_step(step, carry):
+        for j in range(OUTS):
+            total[step * OUTS + j] = jnp.zeros((BLOCK, LANES), jnp.float32)
+        return carry
+
+    lax.fori_loop(0, targets // OUTS, zero_step, 0)
     low_a = low_lanes(HALF)
     low = low_lanes(BLOCK)
 
@@ -164,13 +170,17 @@
     lax.fori_loop(0, steps, chunk_step, 0)
     add(2 * steps - 1, second_ref)
 
-    def out_step(i, carry):
-        value = total[i]
-        value = value + pltpu.roll(value, BLOCK, 1)
-        out_ref[i] = jnp.where(low_a, value[0:HALF], value[HALF:BLOCK])
-        return carry
-
-    lax.fori_loop(0, targets, out_step, 0)
+    def out_step(step, carry):
+        packed = []
+        for j in range(OUTS):
+            value = total[step * OUTS + j]
+            value = value + pltpu.roll(value, BLOCK, 1)
+            packed.append(jnp.where(low_a, value[0:HALF], value[HALF:BLOCK]))
+        for j in range(OUTS):
+            out_ref[step * OUTS + j] = packed[j]
+        return carry
+
+    lax.fori_loop(0, targets // OUTS, out_step, 0)
 
 
 def coarse_kernel(rows, place_ref, ap_ref, p_ref, out_ref, result_ref):
@@ -277,7 +287,7 @@
         scratch_shapes=[
             pltpu.VMEM((columns, 4 * BLOCK, 2 * LANES), jnp.bfloat16),
             pltpu.VMEM((targets + 1, BLOCK, LANES), f32),
-            pltpu.VMEM((2, BLOCK, LANES), f32),
+            pltpu.VMEM((WEIGHTS, 2, BLOCK, LANES), f32),
             pltpu.VMEM((CHUNK * BLOCK, 2 * LANES), f32),
             pltpu.VMEM((CHUNK * BLOCK, 2 * LANES), f32),
         ],

time: 279 us -> 264 us (0.946)
  Pallas kernels: 76.8 us -> 61.7 us
    pallas_call x1, Pallas kernels: 48.4 us -> 33.2 us  [on_device(): pl.pallas_call(functools.partial(ap_kernel, columns, targets), out_shape=...]
  transfers between devices with their start and end apart: 4 -> 4, of which waited for: 3 -> 3; matrix products, arithmetic and copies ran while one was open for 5% -> 6% of each run, Pallas kernels for 7% -> 8%
where the time goes in v3:
time: 264 us
  waiting for transfers between devices  86.6 us (33%)
  blocking collectives  76 us (29%)
  Pallas kernels  61.7 us (23%)
  local copies, waits for them, and re-layouts  14.7 us (6%)
  between operations  13.8 us (5%)
  starting transfers between devices  7.33 us (3%)
  other arithmetic  3.57 us (1%)
    all_to_all x1, blocking collectives, on_device(): lax.all_to_all(outgoing, 'row', split_axis=0, concat_axis=0, tiled=True)  76 us
    reduce_scatter x1, waiting for transfers between devices, on_device(): lax.psum_scatter(partial_ap, 'col', scatter_dimension=0, tiled=True)  37.6 us
    pallas_call x1, Pallas kernels, on_device(): pl.pallas_call(functools.partial(ap_kernel, columns, targets), out_shape=...  33.2 us
    reduce_scatter x1, waiting for transfers between devices, on_device(): lax.psum_scatter(coarse_part, 'col', scatter_dimension=0, tiled=True)  27.6 us
    all_gather x1, waiting for transfers between devices, on_device(): panel = lax.all_gather(p_local, 'row', axis=0, tiled=True)  21.3 us
    pallas_call x1, Pallas kernels, on_device(): pl.pallas_call(functools.partial(plan_kernel, columns, targets), out_shap...  19.8 us
    unnamed x8, local copies, waits for them, and re-layouts  11.6 us
    all_to_all x1, starting transfers between devices, on_device(): lax.all_to_all(meta_send, 'row', split_axis=0, concat_axis=0, tiled=True)  7.25 us
  transfers between devices with their start and end apart: 4, of which 3 were waited for; matrix products, arithmetic and copies ran while one was open for 6% of the time, Pallas kernels for 8%

profile of v3, /device:TPU:0, one launch (start us, length us, event | category | flops | bytes accessed | tf_op | source)
XLA Modules:
  0.0 263.7 jit_solution(5248733740097366766)
XLA Ops:
  6.5 0.0 all-gather.2.cloned.1.call-start
  6.5 1.3 copy.40
  7.8 1.0 reshape.85.p_ref
  8.8 0.0 all-gather.2.cloned.1.call-update
  8.9 0.7 broadcast_multiply_fusion.1
  9.6 0.1 copy.37
  9.6 0.1 mul.43
  9.7 0.8 copy.36
  10.5 0.7 broadcast_multiply_fusion.2
  11.2 0.1 copy.35
  11.3 0.1 mul.41
  11.3 0.1 eq.15
  11.4 0.8 copy.38
  12.3 0.1 reshape.80
  12.3 0.1 copy.39
  12.4 0.2 convert_reduce_fusion
  12.6 1.2 scatter_custom_fusion
  13.8 7.3 %all-to-all-start = ((f32[8,4,6]{2,1,0:T(4,128)}), f32[8,4,6]{2,1,0:T(4,128)S(1)}, u32[]{:S(2)}, u32[]{:S(2)}) async-start(f32[8,4,6]{2,1,0:T(4,128)} %bitcast.2), calls=%async_computation | async-start | bytes 32768 | tf_op jit(solution)/shard_map/all_to_all | solution.py:278
  21.1 0.0 reduce-scatter.3.cloned.1.call-start
  21.1 0.7 broadcast_multiply_fusion
  22.5 0.1 add.43
  22.6 0.7 reduce
  23.3 0.1 reshape.83
  23.4 7.6 %copy.42 = f32[56,8,32,128]{3,2,1,0:T(8,128)} copy(f32[56,8,32,128]{3,1,2,0:T(8,128)} %bitcast.19) | data formatting | bytes 14680064
  31.0 0.6 add.44.target_ref
  31.6 19.8 %plan.1 = (s32[712]{0:T(1024)}, s32[2148]{0:T(1024)}, s32[178]{0:T(256)}, s32[1]{0:T(128)}) custom-call(s32[1]{0:T(128)} %bitcast.17.count_ref, s32[448]{0:T(512)} %bitcast.22, s32[1344]{0:T(1024)} %add.44.target_ref), custom_call_target="tpu_custom_call" | custom-call | bytes 20971520 | tf_op jit(solution)/shard_map/plan/pallas_call | solution.py:257
  51.4 0.0 all-to-all-done
  51.4 0.1 convert_element_type.16.target_ref
  51.5 21.3 %all-gather.2.cloned.1.call-done.panel_ref = f32[192,32,128]{2,1,0:T(8,128)} async-done(((f32[24,32,128]{2,1,0:T(8,128)}), f32[192,32,128]{2,1,0:T(8,128)}) %all-gather.2.cloned.1.call-update) | async-done | bytes 3145744 | tf_op jit(solution)/shard_map/all_gather | solution.py:248
  72.9 33.2 %ap.1 = f32[192,32,128]{2,1,0:T(8,128)} custom-call(s32[1]{0:T(128)} %get-tuple-element.13.chunks_ref, s32[712]{0:T(1024)} %get-tuple-element.14.order_ref, s32[2148]{0:T(1024)} %get-tuple-element.15.place_ref, s32[178]{0:T(256)} %get-tuple-element.16.chunk_ref, f32[448,32,128]{2,1,0:T(8,128)} %bitcast.20, f32[192,32,128]{2,1,0:T(8,128)} %all-gather.2.cloned.1.call-done.panel_ref), custom_call_target="tpu_custom_call" | custom-call | flops 3758096384 | bytes 14680064 | tf_op jit(solution)/shard_map/ap/pallas_call | solution.py:282
  106.1 0.0 copy-start
  106.1 0.0 reduce-scatter.3.cloned.1.call-update
  106.1 0.0 reduce-scatter.5.cloned.1.call-start
  106.1 37.6 %reduce-scatter.3.cloned.1.call-done.ap_ref = f32[48,32,128]{2,1,0:T(8,128)} async-done(((f32[192,32,128]{2,1,0:T(8,128)}), f32[48,32,128]{2,1,0:T(8,128)}) %reduce-scatter.3.cloned.1.call-update) | async-done | bytes 786448 | tf_op jit(solution)/shard_map/reduce_scatter | solution.py:301
  143.8 0.0 copy-done
  143.8 0.0 copy-start.1
  143.8 1.1 copy-done.1
  144.9 3.9 %coarse.1 = f32[192,32,128]{2,1,0:T(8,128)S(1)} custom-call(s32[24]{0:T(128)S(1)} %multiply_add_fusion.place_ref, f32[48,32,128]{2,1,0:T(8,128)S(1)} %copy-done.1, f32[24,32,128]{2,1,0:T(8,128)S(1)} %copy-done), custom_call_target="tpu_custom_call" | custom-call | tf_op jit(solution)/shard_map/coarse/pallas_call | solution.py:303
  148.8 76.0 %all_to_all.14.in_ref = f32[192,32,128]{2,1,0:T(8,128)S(1)} all-to-all(f32[192,32,128]{2,1,0:T(8,128)S(1)} %coarse.1), channel_id=1, replica_groups=mesh['row'=8,'col'=4] {'row'}, dimensions={0} | all-to-all | bytes 6291456 | tf_op jit(solution)/shard_map/all_to_all | solution.py:313
  224.8 4.7 %gather_coarse.1 = f32[108,32,128]{2,1,0:T(8,128)} custom-call(s32[192]{0:T(256)S(1)} %convert_element_type.16.target_ref, f32[192,32,128]{2,1,0:T(8,128)S(1)} %all_to_all.14.in_ref), custom_call_target="tpu_custom_call" | custom-call | tf_op jit(solution)/shard_map/gather_coarse/pallas_call | solution.py:315
  229.6 0.0 reduce-scatter.5.cloned.1.call-update
  229.6 27.6 %reduce-scatter.5.cloned.1.call-done = f32[27,32,128]{2,1,0:T(8,128)} async-done(((f32[108,32,128]{2,1,0:T(8,128)}), f32[27,32,128]{2,1,0:T(8,128)}) %reduce-scatter.5.cloned.1.call-update) | async-done | bytes 442384 | tf_op jit(solution)/shard_map/reduce_scatter | solution.py:324
  (5 shorter events, 0.0 us)
Async XLA Ops:
  6.5 66.3 %all-gather.2.cloned.1.call-start = ((), (), s32[]{:S(2)}) async-start(), calls=%async_computation.4 | async-start | bytes 3538944 | tf_op jit(solution)/shard_map/all_gather | solution.py:248
  13.8 37.6 %all-to-all-start = ((f32[8,4,6]{2,1,0:T(4,128)}), f32[8,4,6]{2,1,0:T(4,128)S(1)}, u32[]{:S(2)}, u32[]{:S(2)}) async-start(f32[8,4,6]{2,1,0:T(4,128)} %bitcast.2), calls=%async_computation | async-start | bytes 32768 | tf_op jit(solution)/shard_map/all_to_all | solution.py:278
  21.1 122.7 %reduce-scatter.3.cloned.1.call-start = ((), (), s32[]{:S(2)}) async-start(), calls=%async_computation.5 | async-start | bytes 3932160 | tf_op jit(solution)/shard_map/reduce_scatter | solution.py:301
  106.1 37.7 %copy-start = (f32[24,32,128]{2,1,0:T(8,128)S(1)}, f32[24,32,128]{2,1,0:T(8,128)}, u32[]{:S(2)}) copy-start(f32[24,32,128]{2,1,0:T(8,128)} %reshape.85.p_ref) | copy-start | bytes 1179652
  106.1 151.1 %reduce-scatter.5.cloned.1.call-start = ((), (), s32[]{:S(2)}) async-start(), calls=%async_computation.6 | async-start | bytes 2211840 | tf_op jit(solution)/shard_map/reduce_scatter | solution.py:324
  143.8 1.1 copy-start.1
Sparse Core Ops, SparseCore 0:
  9.5 63.2 all-gather.1
  106.2 37.4 reduce-scatter.2
  229.7 27.4 reduce-scatter.4

commit v4 on v3

--- a/solution.py
+++ b/solution.py
@@ -13,7 +13,7 @@
 CPD = 1
 TAP = 6
 TC = 27
-CHUNK = 4
+CHUNK = 2
 WEIGHTS = 4
 OUTS = 6
 

time: 264 us -> 273 us (1.034)
  Pallas kernels: 61.7 us -> 71.8 us
    pallas_call x1, Pallas kernels: 33.2 us -> 43 us  [on_device(): pl.pallas_call(functools.partial(ap_kernel, columns, targets), out_shape=...]
  transfers between devices with their start and end apart: 4 -> 4, of which waited for: 3 -> 3; matrix products, arithmetic and copies ran while one was open for 6% -> 5% of each run, Pallas kernels for 8% -> 7%
where the time goes in v4:
time: 273 us
  waiting for transfers between devices  85.2 us (31%)
  blocking collectives  76 us (28%)
  Pallas kernels  71.8 us (26%)
  local copies, waits for them, and re-layouts  14.7 us (5%)
  between operations  13.8 us (5%)
  starting transfers between devices  7.33 us (3%)
  other arithmetic  3.57 us (1%)
    all_to_all x1, blocking collectives, on_device(): lax.all_to_all(outgoing, 'row', split_axis=0, concat_axis=0, tiled=True)  76 us
    pallas_call x1, Pallas kernels, on_device(): pl.pallas_call(functools.partial(ap_kernel, columns, targets), out_shape=...  43 us
    reduce_scatter x1, waiting for transfers between devices, on_device(): lax.psum_scatter(partial_ap, 'col', scatter_dimension=0, tiled=True)  36.5 us
    reduce_scatter x1, waiting for transfers between devices, on_device(): lax.psum_scatter(coarse_part, 'col', scatter_dimension=0, tiled=True)  27.7 us
    all_gather x1, waiting for transfers between devices, on_device(): panel = lax.all_gather(p_local, 'row', axis=0, tiled=True)  20.9 us
    pallas_call x1, Pallas kernels, on_device(): pl.pallas_call(functools.partial(plan_kernel, columns, targets), out_shap...  20.2 us
    unnamed x8, local copies, waits for them, and re-layouts  11.6 us
    all_to_all x1, starting transfers between devices, on_device(): lax.all_to_all(meta_send, 'row', split_axis=0, concat_axis=0, tiled=True)  7.25 us
  transfers between devices with their start and end apart: 4, of which 3 were waited for; matrix products, arithmetic and copies ran while one was open for 5% of the time, Pallas kernels for 7%

profile of v4, /device:TPU:0, one launch (start us, length us, event | category | flops | bytes accessed | tf_op | source)
XLA Modules:
  0.0 272.5 jit_solution(4169681713112614922)
XLA Ops:
  6.5 0.0 all-gather.2.cloned.1.call-start
  6.5 1.3 copy.40
  7.8 1.0 reshape.85.p_ref
  8.8 0.0 all-gather.2.cloned.1.call-update
  8.9 0.7 broadcast_multiply_fusion.1
  9.6 0.1 copy.37
  9.6 0.1 mul.43
  9.7 0.8 copy.36
  10.5 0.7 broadcast_multiply_fusion.2
  11.2 0.1 copy.35
  11.3 0.1 mul.41
  11.3 0.1 eq.15
  11.4 0.8 copy.38
  12.3 0.1 reshape.80
  12.3 0.1 copy.39
  12.4 0.2 convert_reduce_fusion
  12.6 1.2 scatter_custom_fusion
  13.8 7.3 %all-to-all-start = ((f32[8,4,6]{2,1,0:T(4,128)}), f32[8,4,6]{2,1,0:T(4,128)S(1)}, u32[]{:S(2)}, u32[]{:S(2)}) async-start(f32[8,4,6]{2,1,0:T(4,128)} %bitcast.2), calls=%async_computation | async-start | bytes 32768 | tf_op jit(solution)/shard_map/all_to_all | solution.py:278
  21.1 0.0 reduce-scatter.3.cloned.1.call-start
  21.1 0.7 broadcast_multiply_fusion
  22.5 0.1 add.43
  22.6 0.7 reduce
  23.3 0.1 reshape.83
  23.4 7.6 %copy.42 = f32[56,8,32,128]{3,2,1,0:T(8,128)} copy(f32[56,8,32,128]{3,1,2,0:T(8,128)} %bitcast.19) | data formatting | bytes 14680064
  31.0 0.6 add.44.target_ref
  31.6 20.2 %plan.1 = (s32[580]{0:T(1024)}, s32[1746]{0:T(1024)}, s32[290]{0:T(512)}, s32[1]{0:T(128)}) custom-call(s32[1]{0:T(128)} %bitcast.17.count_ref, s32[448]{0:T(512)} %bitcast.22, s32[1344]{0:T(1024)} %add.44.target_ref), custom_call_target="tpu_custom_call" | custom-call | bytes 20971520 | tf_op jit(solution)/shard_map/plan/pallas_call | solution.py:257
  51.8 0.0 all-to-all-done
  51.8 0.1 convert_element_type.16.target_ref
  51.9 20.9 %all-gather.2.cloned.1.call-done.panel_ref = f32[192,32,128]{2,1,0:T(8,128)} async-done(((f32[24,32,128]{2,1,0:T(8,128)}), f32[192,32,128]{2,1,0:T(8,128)}) %all-gather.2.cloned.1.call-update) | async-done | bytes 3145744 | tf_op jit(solution)/shard_map/all_gather | solution.py:248
  72.9 43.0 %ap.1 = f32[192,32,128]{2,1,0:T(8,128)} custom-call(s32[1]{0:T(128)} %get-tuple-element.13.chunks_ref, s32[580]{0:T(1024)} %get-tuple-element.14.order_ref, s32[1746]{0:T(1024)} %get-tuple-element.15.place_ref, s32[290]{0:T(512)} %get-tuple-element.16.chunk_ref, f32[448,32,128]{2,1,0:T(8,128)} %bitcast.20, f32[192,32,128]{2,1,0:T(8,128)} %all-gather.2.cloned.1.call-done.panel_ref), custom_call_target="tpu_custom_call" | custom-call | flops 3758096384 | bytes 14680064 | tf_op jit(solution)/shard_map/ap/pallas_call | solution.py:282
  115.9 0.0 copy-start
  115.9 0.0 reduce-scatter.3.cloned.1.call-update
  115.9 0.0 reduce-scatter.5.cloned.1.call-start
  116.0 36.5 %reduce-scatter.3.cloned.1.call-done.ap_ref = f32[48,32,128]{2,1,0:T(8,128)} async-done(((f32[192,32,128]{2,1,0:T(8,128)}), f32[48,32,128]{2,1,0:T(8,128)}) %reduce-scatter.3.cloned.1.call-update) | async-done | bytes 786448 | tf_op jit(solution)/shard_map/reduce_scatter | solution.py:301
  152.5 0.0 copy-done
  152.5 0.0 copy-start.1
  152.5 1.1 copy-done.1
  153.7 3.9 %coarse.1 = f32[192,32,128]{2,1,0:T(8,128)S(1)} custom-call(s32[24]{0:T(128)S(1)} %multiply_add_fusion.place_ref, f32[48,32,128]{2,1,0:T(8,128)S(1)} %copy-done.1, f32[24,32,128]{2,1,0:T(8,128)S(1)} %copy-done), custom_call_target="tpu_custom_call" | custom-call | tf_op jit(solution)/shard_map/coarse/pallas_call | solution.py:303
  157.6 76.0 %all_to_all.14.in_ref = f32[192,32,128]{2,1,0:T(8,128)S(1)} all-to-all(f32[192,32,128]{2,1,0:T(8,128)S(1)} %coarse.1), channel_id=1, replica_groups=mesh['row'=8,'col'=4] {'row'}, dimensions={0} | all-to-all | bytes 6291456 | tf_op jit(solution)/shard_map/all_to_all | solution.py:313
  233.6 4.7 %gather_coarse.1 = f32[108,32,128]{2,1,0:T(8,128)} custom-call(s32[192]{0:T(256)S(1)} %convert_element_type.16.target_ref, f32[192,32,128]{2,1,0:T(8,128)S(1)} %all_to_all.14.in_ref), custom_call_target="tpu_custom_call" | custom-call | tf_op jit(solution)/shard_map/gather_coarse/pallas_call | solution.py:315
  238.3 0.0 reduce-scatter.5.cloned.1.call-update
  238.3 27.7 %reduce-scatter.5.cloned.1.call-done = f32[27,32,128]{2,1,0:T(8,128)} async-done(((f32[108,32,128]{2,1,0:T(8,128)}), f32[27,32,128]{2,1,0:T(8,128)}) %reduce-scatter.5.cloned.1.call-update) | async-done | bytes 442384 | tf_op jit(solution)/shard_map/reduce_scatter | solution.py:324
  (5 shorter events, 0.0 us)
Async XLA Ops:
  6.5 66.3 %all-gather.2.cloned.1.call-start = ((), (), s32[]{:S(2)}) async-start(), calls=%async_computation.4 | async-start | bytes 3538944 | tf_op jit(solution)/shard_map/all_gather | solution.py:248
  13.8 38.0 %all-to-all-start = ((f32[8,4,6]{2,1,0:T(4,128)}), f32[8,4,6]{2,1,0:T(4,128)S(1)}, u32[]{:S(2)}, u32[]{:S(2)}) async-start(f32[8,4,6]{2,1,0:T(4,128)} %bitcast.2), calls=%async_computation | async-start | bytes 32768 | tf_op jit(solution)/shard_map/all_to_all | solution.py:278
  21.1 131.4 %reduce-scatter.3.cloned.1.call-start = ((), (), s32[]{:S(2)}) async-start(), calls=%async_computation.5 | async-start | bytes 3932160 | tf_op jit(solution)/shard_map/reduce_scatter | solution.py:301
  115.9 36.6 %copy-start = (f32[24,32,128]{2,1,0:T(8,128)S(1)}, f32[24,32,128]{2,1,0:T(8,128)}, u32[]{:S(2)}) copy-start(f32[24,32,128]{2,1,0:T(8,128)} %reshape.85.p_ref) | copy-start | bytes 1179652
  115.9 150.1 %reduce-scatter.5.cloned.1.call-start = ((), (), s32[]{:S(2)}) async-start(), calls=%async_computation.6 | async-start | bytes 2211840 | tf_op jit(solution)/shard_map/reduce_scatter | solution.py:324
  152.5 1.1 copy-start.1
Sparse Core Ops, SparseCore 0:
  9.5 63.2 all-gather.1
  116.0 36.4 reduce-scatter.2
  238.4 27.5 reduce-scatter.4
